TPU v7x, 32 devices: a whole 2x2x4 slice. The times are simulated.
32 devices in a mesh: ctx: 8 (over z, y), head: 4 (over x, core).
Axes of the slice: x: 2, y: 2, z: 4, core: 2. Of those that a mesh axis runs over, the one named last changes fastest.
Arguments:
- long_q: bfloat16 [4096, 8192], P(('ctx', 'head')), may hold values from -5 to 5
- long_kv: bfloat16 [4096, 2048], P(('ctx', 'head')), may hold values from -5 to 5
- long_lengths: int32 [4], replicated, may hold values from 1 to 2048, 4096 in all
- short_q: bfloat16 [1024, 8192], P(('ctx', 'head')), may hold values from -5 to 5
- short_kv: bfloat16 [1024, 2048], P(('ctx', 'head')), may hold values from -5 to 5
- short_docs: int32 [32, 32], P('ctx'), may hold values from 0 to 3, never falling along the last dimension, each value on 1 to 16 neighbouring positions
- short_dest: int32 [8, 4], P('ctx'), may hold values from 0 to 7, as said below
Outputs:
- long_out: bfloat16 [4096, 8192], P(('ctx', 'head'))
- short_out: bfloat16 [2048, 8192], P('ctx', 'head')
Inputs may be any that keep to these rules, and one draw needn't show every extreme that they name: `long_lengths`: they sum to 4096; the largest is exactly 2048. `short_docs`: each row of 32 positions holds documents 0 to 3 in order, each of 1 to 16 positions, one of exactly 16. `short_dest`: row s lists the destinations of the 4 groups of ctx index s; the entries of a row are all different.
All inputs are finite; a program needn't handle non-finite values.
Results may differ from a plain program's by a relative error of at most 0.0065.
Values may be sent and summed in bfloat16 or wider, within the bound.
A program may use at most 128 MiB of HBM per device.

v0:
```python
import math

import jax
import jax.numpy as jnp
from jax import lax
from jax.sharding import PartitionSpec as P

H = 64
KV = 8
HD = 128
SCAP = 32


masked_score = -1e30


def doc_numbers(doc_ends, positions):
    return jnp.sum((positions[:, None] >= doc_ends[None, :]).astype(jnp.int32), axis=1)


def block_step(attn_state, kv_block, key_pos, context):
    queries, query_pos, query_doc, doc_ends = context
    key_doc = doc_numbers(doc_ends, key_pos)
    visible = (
        (query_doc[:, None] == key_doc[None, :])
        & (key_pos[None, :] <= query_pos[:, None])
        & (key_pos[None, :] >= 0)
    )
    kv_count = queries.shape[1]

    def update(current):
        row_top, denominator, numerator = current
        key_value = kv_block.reshape(kv_block.shape[0], kv_count, 2, HD)
        scores = jnp.einsum(
            "qhgd,khd->qhgk", queries, key_value[:, :, 0], preferred_element_type=jnp.float32
        ) * HD ** (-0.5)
        scores = jnp.where(visible[:, None, None, :], scores, masked_score)
        new_top = jnp.maximum(row_top, jnp.max(scores, axis=-1))
        weight = jnp.where(visible[:, None, None, :], jnp.exp(scores - new_top[..., None]), 0.0)
        factor = jnp.exp(row_top - new_top)
        denominator = denominator * factor + jnp.sum(weight, axis=-1)
        numerator = numerator * factor[..., None] + jnp.einsum(
            "qhgk,khd->qhgd",
            weight.astype(jnp.bfloat16),
            key_value[:, :, 1],
            preferred_element_type=jnp.float32,
        )
        return (new_top, denominator, numerator)

    def keep(current):
        return current

    return lax.cond(jnp.any(visible), update, keep, attn_state)


def run_piece(attn_state, kv_piece, key_pos, context):
    row_count = kv_piece.shape[0]
    block_rows = math.gcd(row_count, 256)
    block_count = row_count // block_rows
    blocks = kv_piece.reshape(block_count, block_rows, kv_piece.shape[1])
    block_pos = key_pos.reshape(block_count, block_rows)

    def scan_step(current, inputs):
        return (block_step(current, inputs[0], inputs[1], context), None)

    final_state, unused = lax.scan(scan_step, attn_state, (blocks, block_pos))
    return final_state


def short_attend(queries, kv_rows, doc_ids, kv_count, group_size):
    row_count = queries.shape[0]
    block_rows = math.gcd(row_count, 128)
    block_count = row_count // block_rows
    query_blocks = queries.reshape(block_count, block_rows, kv_count, group_size, HD)
    kv_blocks = kv_rows.reshape(block_count, block_rows, kv_count, 2, HD)
    offsets = jnp.arange(block_rows, dtype=jnp.int32)
    group_ids = offsets // SCAP
    doc_block = doc_ids.reshape(block_count, block_rows)
    visible = (doc_block[:, :, None] == doc_block[:, None, :]) & (
        (group_ids[:, None] == group_ids[None, :]) & (offsets[None, :] <= offsets[:, None])
    )[None]
    scores = jnp.einsum(
        "bqhgd,bkhd->bqhgk", query_blocks, kv_blocks[:, :, :, 0], preferred_element_type=jnp.float32
    ) * HD ** (-0.5)
    scores = jnp.where(visible[:, :, None, None, :], scores, masked_score)
    row_top = jnp.max(scores, axis=-1, keepdims=True)
    weight = jnp.where(visible[:, :, None, None, :], jnp.exp(scores - row_top), 0.0)
    denominator = jnp.sum(weight, axis=-1)
    numerator = jnp.einsum(
        "bqhgk,bkhd->bqhgd",
        weight.astype(jnp.bfloat16),
        kv_blocks[:, :, :, 1],
        preferred_element_type=jnp.float32,
    )
    return (
        (numerator / denominator[..., None])
        .astype(jnp.bfloat16)
        .reshape(row_count, kv_count * group_size * HD)
    )


def place_groups(selector, rows_array, groups):
    shaped = rows_array.reshape(groups, rows_array.shape[0] // groups, rows_array.shape[1])
    return jnp.einsum("eg,grc->erc", selector, shaped, preferred_element_type=jnp.float32).astype(
        jnp.bfloat16
    )


def per_device(long_q, long_kv, long_lengths, short_q, short_kv, short_docs, short_dest):
    head_count = lax.axis_size("head")
    ctx_count = lax.axis_size("ctx")
    kv_count = KV // head_count
    group_size = H // KV
    q_long, kv_long, q_short, kv_short = (
        lax.all_to_all(long_q, "head", split_axis=1, concat_axis=0, tiled=True),
        lax.all_to_all(long_kv, "head", split_axis=1, concat_axis=0, tiled=True),
        lax.all_to_all(short_q, "head", split_axis=1, concat_axis=0, tiled=True),
        lax.all_to_all(short_kv, "head", split_axis=1, concat_axis=0, tiled=True),
    )
    row_count = q_long.shape[0]
    ctx_rank = lax.axis_index("ctx")
    doc_ends = jnp.cumsum(long_lengths)
    query_pos = ctx_rank * row_count + jnp.arange(row_count, dtype=jnp.int32)
    query_doc = doc_numbers(doc_ends, query_pos)
    queries = q_long.reshape(row_count, kv_count, group_size, HD)
    context = (queries, query_pos, query_doc, doc_ends)
    start_state = (
        jnp.full((row_count, kv_count, group_size), masked_score, jnp.float32),
        jnp.zeros((row_count, kv_count, group_size), jnp.float32),
        jnp.zeros((row_count, kv_count, group_size, HD), jnp.float32),
    )
    kv_piece = lax.all_gather(kv_long, "ctx", axis=0, tiled=True)
    key_pos = jnp.arange(kv_piece.shape[0], dtype=jnp.int32)
    attn_state = run_piece(start_state, kv_piece, key_pos, context)
    long_att = (
        (attn_state[2] / attn_state[1][..., None])
        .astype(jnp.bfloat16)
        .reshape(row_count, kv_count * group_size * HD)
    )
    long_out = lax.all_to_all(long_att, "head", split_axis=0, concat_axis=1, tiled=True)
    groups = short_docs.shape[0]
    targets = short_dest[0]
    selector = (targets[None, :] == jnp.arange(ctx_count, dtype=jnp.int32)[:, None]).astype(
        jnp.bfloat16
    )
    send_q = place_groups(selector, q_short, groups)
    send_kv = place_groups(selector, kv_short, groups)
    send_docs = jnp.einsum(
        "eg,gr->er", selector, short_docs.astype(jnp.bfloat16), preferred_element_type=jnp.float32
    ).astype(jnp.bfloat16)
    arrived_q, arrived_kv, arrived_docs = (
        lax.all_to_all(send_q, "ctx", split_axis=0, concat_axis=0, tiled=True),
        lax.all_to_all(send_kv, "ctx", split_axis=0, concat_axis=0, tiled=True),
        lax.all_to_all(send_docs, "ctx", split_axis=0, concat_axis=0, tiled=True),
    )
    short_out = short_attend(
        arrived_q.reshape(-1, arrived_q.shape[-1]),
        arrived_kv.reshape(-1, arrived_kv.shape[-1]),
        arrived_docs.reshape(-1).astype(jnp.int32),
        kv_count,
        group_size,
    )
    return (long_out, short_out)


def solution(mesh):
    in_specs = (
        P(("ctx", "head"), None),
        P(("ctx", "head"), None),
        P(),
        P(("ctx", "head"), None),
        P(("ctx", "head"), None),
        P("ctx", None),
        P("ctx", None),
    )
    out_specs = (P(("ctx", "head"), None), P("ctx", "head"))
    return jax.shard_map(
        per_device, mesh=mesh, in_specs=in_specs, out_specs=out_specs, check_vma=False
    )
```

profile of v0, /device:TPU:12, one launch (start us, length us, event | category | flops | bytes accessed | tf_op | source)
XLA Modules:
  0.0 276.2 jit_solution(3412407050726507432)
XLA Ops:
  8.7 11.4 %all_to_all.105 = bf16[128,4,512]{0,2,1:T(8,128)(2,1)S(1)} all-to-all(bf16[128,4,512]{0,2,1:T(8,128)(2,1)S(1)} %bitcast.126), channel_id=1, replica_groups=mesh['ctx'=8,'head'=4] {'head'}, dimensions={1} | all-to-all | bytes 1048576 | tf_op jit(solution)/shard_map/all_to_all | solution.py:116
  22.7 6.2 %all-to-all-start.5 = ((bf16[8,1,32]{2,1,0:T(2,128)(2,1)}), bf16[8,1,32]{2,1,0:T(2,128)(2,1)S(1)}, u32[]{:S(2)}, u32[]{:S(2)}) async-start(bf16[8,1,32]{2,1,0:T(2,128)(2,1)} %copy.118), calls=%async_computation.5 | async-start | bytes 8192 | tf_op jit(solution)/shard_map/all_to_all | solution.py:154
  32.9 3.3 %all-to-all-start.3 = ((bf16[32,4,512]{2,0,1:T(8,128)(2,1)}), bf16[32,4,512]{2,0,1:T(8,128)(2,1)S(1)}, u32[]{:S(2)}, u32[]{:S(2)}) async-start(bf16[32,4,512]{2,0,1:T(8,128)(2,1)} %bitcast.111), calls=%async_computation.3 | async-start | bytes 262144 | tf_op jit(solution)/shard_map/all_to_all | solution.py:118
  40.9 3.5 %all-to-all-start.6 = ((bf16[32,4,2048]{2,0,1:T(8,128)(2,1)}), bf16[32,4,2048]{2,0,1:T(8,128)(2,1)S(1)}, u32[]{:S(2)}, u32[]{:S(2)}) async-start(bf16[32,4,2048]{2,0,1:T(8,128)(2,1)} %bitcast.110), calls=%async_computation.6 | async-start | bytes 1048576 | tf_op jit(solution)/shard_map/all_to_all | solution.py:117
  45.8 7.3 %all-to-all-done.6 = bf16[32,4,2048]{2,0,1:T(8,128)(2,1)S(1)} async-done(((bf16[32,4,2048]{2,0,1:T(8,128)(2,1)}), bf16[32,4,2048]{2,0,1:T(8,128)(2,1)S(1)}, u32[]{:S(2)}, u32[]{:S(2)}) %all-to-all-start.6) | async-done | bytes 524320 | tf_op jit(solution)/shard_map/all_to_all | solution.py:117
  53.2 3.8 %all-to-all-start.1 = ((bf16[128,4,2048]{2,0,1:T(8,128)(2,1)}), bf16[128,4,2048]{2,0,1:T(8,128)(2,1)S(1)}, u32[]{:S(2)}, u32[]{:S(2)}) async-start(bf16[128,4,2048]{2,0,1:T(8,128)(2,1)} %bitcast.118), calls=%async_computation.1 | async-start | bytes 4194304 | tf_op jit(solution)/shard_map/all_to_all | solution.py:115
  58.3 24.3 %all-to-all-done.1 = bf16[128,4,2048]{2,0,1:T(8,128)(2,1)S(1)} async-done(((bf16[128,4,2048]{2,0,1:T(8,128)(2,1)}), bf16[128,4,2048]{2,0,1:T(8,128)(2,1)S(1)}, u32[]{:S(2)}, u32[]{:S(2)}) %all-to-all-start.1) | async-done | bytes 2097184 | tf_op jit(solution)/shard_map/all_to_all | solution.py:115
  82.6 5.6 %all-to-all-start.4 = ((bf16[8,32,512]{2,1,0:T(8,128)(2,1)}), bf16[8,32,512]{2,1,0:T(8,128)(2,1)S(1)}, u32[]{:S(2)}, u32[]{:S(2)}) async-start(bf16[8,32,512]{2,1,0:T(8,128)(2,1)} %copy.116), calls=%async_computation.4 | async-start | bytes 524288 | tf_op jit(solution)/shard_map/all_to_all | solution.py:153
  91.7 2.9 %all-gather.2.cloned.1.call-done = bf16[4096,512]{1,0:T(8,128)(2,1)} async-done(((bf16[512,512]{1,0:T(8,128)(2,1)}), bf16[4096,512]{1,0:T(8,128)(2,1)}) %all-gather.2.cloned.1.call-update) | async-done | bytes 4194320 | tf_op jit(solution)/shard_map/all_gather | solution.py:132
  94.5 6.4 %copy.110 = bf16[16,256,512]{1,2,0:T(8,128)(2,1)} copy(bf16[16,256,512]{2,1,0:T(8,128)(2,1)} %bitcast.121) | data formatting | bytes 8388608
  101.6 8.3 %all-to-all-start.7 = ((bf16[8,32,2048]{2,1,0:T(8,128)(2,1)}), bf16[8,32,2048]{2,1,0:T(8,128)(2,1)S(1)}, u32[]{:S(2)}, u32[]{:S(2)}) async-start(bf16[8,32,2048]{2,1,0:T(8,128)(2,1)} %copy.122), calls=%async_computation.7 | async-start | bytes 2097152 | tf_op jit(solution)/shard_map/all_to_all | solution.py:152
  112.4 114.1 %while.15 = (s32[]{:T(128)}, f32[512,2,8]{0,2,1:T(8,128)S(1)}, f32[512,2,8]{0,2,1:T(8,128)S(1)}, f32[512,2,8,128]{3,0,2,1:T(8,128)}, s32[512]{0:T(512)S(1)}, /*i...) while((s32[]{:T(128)}, f32[512,2,8]{0,2,1:T(8,128)S(1)}, ...), condition=%wide.region_9.10_spmd.clone, body=%wide.region_2.9_spmd.clone.sunk | while | flops 1103777280 | bytes 71054144 | solution.py:66
  113.9 11.2 %conditional.3 = ((f32[512,2,8]{0,2,1:T(8,128)S(1)}, f32[512,2,8]{0,2,1:T(8,128)S(1)}, f32[512,2,8,128]{3,0,2,1:T(8,128)})) conditional(s32[]{:T(128)} %convert_element_type.83, (f32[512,2,8]{0,2,1:T(8,128)S(1)}, f32[512,2,8]{0,2,1:T(8,128)S(1)}, f32[512,2,8,128]{3,0,2,1:T(8,128)}) %tuple.60, (pred[512,256]{0,1:T(8,128)(4,1)S(1)}, ...), branch_computations={%region_5.5_spmd, %region_6.8_spmd} | conditional | flops 1103118336 | bytes 70910048 | solution.py:53
  118.7 4.4 %bitcast_add_fusion = f32[512,2,8,128]{3,0,2,1:T(8,128)S(1)} fusion(f32[512,2,8,128]{3,0,2,1:T(8,128)S(1)} %copy-done, f32[512,2,8]{0,2,1:T(8,128)S(1)} %get-tuple-element.221, f32[2,256,512,8]{2,1,3,0:T(8,128)S(1)} %get-tuple-element.227, f32[512,2,8]{0,2,1:T(8,128)S(1)} %max.3, pred[512,256]{0,1:T(8,128)(4,1)S(1)} %get-tuple-element.78, ...), kind=kOutput, calls=%fused_computation.7 | convolution fusion | flops 549453824 | bytes 17104896 | tf_op jit(solution)/shard_map/while/body/eval_jaxpr/cond/branch_1_fun/qhgk,khd->qhgd/dot_general | solution.py:42
  126.6 11.2 %conditional.3 = ((f32[512,2,8]{0,2,1:T(8,128)S(1)}, f32[512,2,8]{0,2,1:T(8,128)S(1)}, f32[512,2,8,128]{3,0,2,1:T(8,128)})) conditional(s32[]{:T(128)} %convert_element_type.83, (f32[512,2,8]{0,2,1:T(8,128)S(1)}, f32[512,2,8]{0,2,1:T(8,128)S(1)}, f32[512,2,8,128]{3,0,2,1:T(8,128)}) %tuple.60, (pred[512,256]{0,1:T(8,128)(4,1)S(1)}, ...), branch_computations={%region_5.5_spmd, %region_6.8_spmd} | conditional | flops 1103118336 | bytes 70910048 | solution.py:53
  131.4 4.4 %bitcast_add_fusion = f32[512,2,8,128]{3,0,2,1:T(8,128)S(1)} fusion(f32[512,2,8,128]{3,0,2,1:T(8,128)S(1)} %copy-done, f32[512,2,8]{0,2,1:T(8,128)S(1)} %get-tuple-element.221, f32[2,256,512,8]{2,1,3,0:T(8,128)S(1)} %get-tuple-element.227, f32[512,2,8]{0,2,1:T(8,128)S(1)} %max.3, pred[512,256]{0,1:T(8,128)(4,1)S(1)} %get-tuple-element.78, ...), kind=kOutput, calls=%fused_computation.7 | convolution fusion | flops 549453824 | bytes 17104896 | tf_op jit(solution)/shard_map/while/body/eval_jaxpr/cond/branch_1_fun/qhgk,khd->qhgd/dot_general | solution.py:42
  139.3 11.2 %conditional.3 = ((f32[512,2,8]{0,2,1:T(8,128)S(1)}, f32[512,2,8]{0,2,1:T(8,128)S(1)}, f32[512,2,8,128]{3,0,2,1:T(8,128)})) conditional(s32[]{:T(128)} %convert_element_type.83, (f32[512,2,8]{0,2,1:T(8,128)S(1)}, f32[512,2,8]{0,2,1:T(8,128)S(1)}, f32[512,2,8,128]{3,0,2,1:T(8,128)}) %tuple.60, (pred[512,256]{0,1:T(8,128)(4,1)S(1)}, ...), branch_computations={%region_5.5_spmd, %region_6.8_spmd} | conditional | flops 1103118336 | bytes 70910048 | solution.py:53
  144.2 4.4 %bitcast_add_fusion = f32[512,2,8,128]{3,0,2,1:T(8,128)S(1)} fusion(f32[512,2,8,128]{3,0,2,1:T(8,128)S(1)} %copy-done, f32[512,2,8]{0,2,1:T(8,128)S(1)} %get-tuple-element.221, f32[2,256,512,8]{2,1,3,0:T(8,128)S(1)} %get-tuple-element.227, f32[512,2,8]{0,2,1:T(8,128)S(1)} %max.3, pred[512,256]{0,1:T(8,128)(4,1)S(1)} %get-tuple-element.78, ...), kind=kOutput, calls=%fused_computation.7 | convolution fusion | flops 549453824 | bytes 17104896 | tf_op jit(solution)/shard_map/while/body/eval_jaxpr/cond/branch_1_fun/qhgk,khd->qhgd/dot_general | solution.py:42
  152.0 11.2 %conditional.3 = ((f32[512,2,8]{0,2,1:T(8,128)S(1)}, f32[512,2,8]{0,2,1:T(8,128)S(1)}, f32[512,2,8,128]{3,0,2,1:T(8,128)})) conditional(s32[]{:T(128)} %convert_element_type.83, (f32[512,2,8]{0,2,1:T(8,128)S(1)}, f32[512,2,8]{0,2,1:T(8,128)S(1)}, f32[512,2,8,128]{3,0,2,1:T(8,128)}) %tuple.60, (pred[512,256]{0,1:T(8,128)(4,1)S(1)}, ...), branch_computations={%region_5.5_spmd, %region_6.8_spmd} | conditional | flops 1103118336 | bytes 70910048 | solution.py:53
  156.9 4.4 %bitcast_add_fusion = f32[512,2,8,128]{3,0,2,1:T(8,128)S(1)} fusion(f32[512,2,8,128]{3,0,2,1:T(8,128)S(1)} %copy-done, f32[512,2,8]{0,2,1:T(8,128)S(1)} %get-tuple-element.221, f32[2,256,512,8]{2,1,3,0:T(8,128)S(1)} %get-tuple-element.227, f32[512,2,8]{0,2,1:T(8,128)S(1)} %max.3, pred[512,256]{0,1:T(8,128)(4,1)S(1)} %get-tuple-element.78, ...), kind=kOutput, calls=%fused_computation.7 | convolution fusion | flops 549453824 | bytes 17104896 | tf_op jit(solution)/shard_map/while/body/eval_jaxpr/cond/branch_1_fun/qhgk,khd->qhgd/dot_general | solution.py:42
  164.7 11.2 %conditional.3 = ((f32[512,2,8]{0,2,1:T(8,128)S(1)}, f32[512,2,8]{0,2,1:T(8,128)S(1)}, f32[512,2,8,128]{3,0,2,1:T(8,128)})) conditional(s32[]{:T(128)} %convert_element_type.83, (f32[512,2,8]{0,2,1:T(8,128)S(1)}, f32[512,2,8]{0,2,1:T(8,128)S(1)}, f32[512,2,8,128]{3,0,2,1:T(8,128)}) %tuple.60, (pred[512,256]{0,1:T(8,128)(4,1)S(1)}, ...), branch_computations={%region_5.5_spmd, %region_6.8_spmd} | conditional | flops 1103118336 | bytes 70910048 | solution.py:53
  169.6 4.4 %bitcast_add_fusion = f32[512,2,8,128]{3,0,2,1:T(8,128)S(1)} fusion(f32[512,2,8,128]{3,0,2,1:T(8,128)S(1)} %copy-done, f32[512,2,8]{0,2,1:T(8,128)S(1)} %get-tuple-element.221, f32[2,256,512,8]{2,1,3,0:T(8,128)S(1)} %get-tuple-element.227, f32[512,2,8]{0,2,1:T(8,128)S(1)} %max.3, pred[512,256]{0,1:T(8,128)(4,1)S(1)} %get-tuple-element.78, ...), kind=kOutput, calls=%fused_computation.7 | convolution fusion | flops 549453824 | bytes 17104896 | tf_op jit(solution)/shard_map/while/body/eval_jaxpr/cond/branch_1_fun/qhgk,khd->qhgd/dot_general | solution.py:42
  177.4 11.2 %conditional.3 = ((f32[512,2,8]{0,2,1:T(8,128)S(1)}, f32[512,2,8]{0,2,1:T(8,128)S(1)}, f32[512,2,8,128]{3,0,2,1:T(8,128)})) conditional(s32[]{:T(128)} %convert_element_type.83, (f32[512,2,8]{0,2,1:T(8,128)S(1)}, f32[512,2,8]{0,2,1:T(8,128)S(1)}, f32[512,2,8,128]{3,0,2,1:T(8,128)}) %tuple.60, (pred[512,256]{0,1:T(8,128)(4,1)S(1)}, ...), branch_computations={%region_5.5_spmd, %region_6.8_spmd} | conditional | flops 1103118336 | bytes 70910048 | solution.py:53
  182.3 4.4 %bitcast_add_fusion = f32[512,2,8,128]{3,0,2,1:T(8,128)S(1)} fusion(f32[512,2,8,128]{3,0,2,1:T(8,128)S(1)} %copy-done, f32[512,2,8]{0,2,1:T(8,128)S(1)} %get-tuple-element.221, f32[2,256,512,8]{2,1,3,0:T(8,128)S(1)} %get-tuple-element.227, f32[512,2,8]{0,2,1:T(8,128)S(1)} %max.3, pred[512,256]{0,1:T(8,128)(4,1)S(1)} %get-tuple-element.78, ...), kind=kOutput, calls=%fused_computation.7 | convolution fusion | flops 549453824 | bytes 17104896 | tf_op jit(solution)/shard_map/while/body/eval_jaxpr/cond/branch_1_fun/qhgk,khd->qhgd/dot_general | solution.py:42
  190.1 11.2 %conditional.3 = ((f32[512,2,8]{0,2,1:T(8,128)S(1)}, f32[512,2,8]{0,2,1:T(8,128)S(1)}, f32[512,2,8,128]{3,0,2,1:T(8,128)})) conditional(s32[]{:T(128)} %convert_element_type.83, (f32[512,2,8]{0,2,1:T(8,128)S(1)}, f32[512,2,8]{0,2,1:T(8,128)S(1)}, f32[512,2,8,128]{3,0,2,1:T(8,128)}) %tuple.60, (pred[512,256]{0,1:T(8,128)(4,1)S(1)}, ...), branch_computations={%region_5.5_spmd, %region_6.8_spmd} | conditional | flops 1103118336 | bytes 70910048 | solution.py:53
  195.0 4.4 %bitcast_add_fusion = f32[512,2,8,128]{3,0,2,1:T(8,128)S(1)} fusion(f32[512,2,8,128]{3,0,2,1:T(8,128)S(1)} %copy-done, f32[512,2,8]{0,2,1:T(8,128)S(1)} %get-tuple-element.221, f32[2,256,512,8]{2,1,3,0:T(8,128)S(1)} %get-tuple-element.227, f32[512,2,8]{0,2,1:T(8,128)S(1)} %max.3, pred[512,256]{0,1:T(8,128)(4,1)S(1)} %get-tuple-element.78, ...), kind=kOutput, calls=%fused_computation.7 | convolution fusion | flops 549453824 | bytes 17104896 | tf_op jit(solution)/shard_map/while/body/eval_jaxpr/cond/branch_1_fun/qhgk,khd->qhgd/dot_general | solution.py:42
  202.8 11.2 %conditional.3 = ((f32[512,2,8]{0,2,1:T(8,128)S(1)}, f32[512,2,8]{0,2,1:T(8,128)S(1)}, f32[512,2,8,128]{3,0,2,1:T(8,128)})) conditional(s32[]{:T(128)} %convert_element_type.83, (f32[512,2,8]{0,2,1:T(8,128)S(1)}, f32[512,2,8]{0,2,1:T(8,128)S(1)}, f32[512,2,8,128]{3,0,2,1:T(8,128)}) %tuple.60, (pred[512,256]{0,1:T(8,128)(4,1)S(1)}, ...), branch_computations={%region_5.5_spmd, %region_6.8_spmd} | conditional | flops 1103118336 | bytes 70910048 | solution.py:53
  207.7 4.4 %bitcast_add_fusion = f32[512,2,8,128]{3,0,2,1:T(8,128)S(1)} fusion(f32[512,2,8,128]{3,0,2,1:T(8,128)S(1)} %copy-done, f32[512,2,8]{0,2,1:T(8,128)S(1)} %get-tuple-element.221, f32[2,256,512,8]{2,1,3,0:T(8,128)S(1)} %get-tuple-element.227, f32[512,2,8]{0,2,1:T(8,128)S(1)} %max.3, pred[512,256]{0,1:T(8,128)(4,1)S(1)} %get-tuple-element.78, ...), kind=kOutput, calls=%fused_computation.7 | convolution fusion | flops 549453824 | bytes 17104896 | tf_op jit(solution)/shard_map/while/body/eval_jaxpr/cond/branch_1_fun/qhgk,khd->qhgd/dot_general | solution.py:42
  226.5 2.9 %divide_convert_fusion = bf16[512,2,8,128]{3,0,2,1:T(8,128)(2,1)S(1)} fusion(f32[512,2,8,128]{3,0,2,1:T(8,128)} %get-tuple-element.102, f32[512,2,8]{0,2,1:T(8,128)S(1)} %get-tuple-element.103), kind=kLoop, calls=%fused_computation.28 | loop fusion | flops 2097152 | bytes 6324224 | tf_op jit(solution)/shard_map/convert_element_type | solution.py:137
  233.0 4.2 %all-to-all-start.2 = ((bf16[4,128,2048]{2,1,0:T(8,128)(2,1)}), bf16[4,128,2048]{2,1,0:T(8,128)(2,1)S(1)}, u32[]{:S(2)}, u32[]{:S(2)}) async-start(bf16[4,128,2048]{2,1,0:T(8,128)(2,1)} %all_to_all.83), calls=%async_computation.2 | async-start | bytes 4194304 | tf_op jit(solution)/shard_map/all_to_all | solution.py:140
  249.5 13.4 %all-to-all-done.2 = bf16[4,128,2048]{2,1,0:T(8,128)(2,1)S(1)} async-done(((bf16[4,128,2048]{2,1,0:T(8,128)(2,1)}), bf16[4,128,2048]{2,1,0:T(8,128)(2,1)S(1)}, u32[]{:S(2)}, u32[]{:S(2)}) %all-to-all-start.2) | async-done | bytes 2097184 | tf_op jit(solution)/shard_map/all_to_all | solution.py:140
  265.3 4.1 %copy.126 = bf16[128,8192]{1,0:T(8,128)(2,1)} copy(bf16[128,8192]{0,1:T(8,128)(2,1)} %bitcast.120) | data formatting | bytes 4194304
  (202 shorter events, 109.6 us)
Async XLA Ops:
  7.2 37.2 %copy-start.2 = (bf16[128,8192]{1,0:T(8,128)(2,1)S(1)}, bf16[128,8192]{1,0:T(8,128)(2,1)}, u32[]{:S(2)}) copy-start(bf16[128,8192]{1,0:T(8,128)(2,1)} %param.11) | copy-start | bytes 6291460
  7.2 87.3 %all-gather.2.cloned.1.call-start = ((), (), s32[]{:S(2)}) async-start(), calls=%async_computation.8 | async-start | bytes 4718592 | tf_op jit(solution)/shard_map/all_gather | solution.py:132
  22.7 10.3 %all-to-all-start.5 = ((bf16[8,1,32]{2,1,0:T(2,128)(2,1)}), bf16[8,1,32]{2,1,0:T(2,128)(2,1)S(1)}, u32[]{:S(2)}, u32[]{:S(2)}) async-start(bf16[8,1,32]{2,1,0:T(2,128)(2,1)} %copy.118), calls=%async_computation.5 | async-start | bytes 8192 | tf_op jit(solution)/shard_map/all_to_all | solution.py:154
  32.9 7.9 %all-to-all-start.3 = ((bf16[32,4,512]{2,0,1:T(8,128)(2,1)}), bf16[32,4,512]{2,0,1:T(8,128)(2,1)S(1)}, u32[]{:S(2)}, u32[]{:S(2)}) async-start(bf16[32,4,512]{2,0,1:T(8,128)(2,1)} %bitcast.111), calls=%async_computation.3 | async-start | bytes 262144 | tf_op jit(solution)/shard_map/all_to_all | solution.py:118
  40.9 12.3 %all-to-all-start.6 = ((bf16[32,4,2048]{2,0,1:T(8,128)(2,1)}), bf16[32,4,2048]{2,0,1:T(8,128)(2,1)S(1)}, u32[]{:S(2)}, u32[]{:S(2)}) async-start(bf16[32,4,2048]{2,0,1:T(8,128)(2,1)} %bitcast.110), calls=%async_computation.6 | async-start | bytes 1048576 | tf_op jit(solution)/shard_map/all_to_all | solution.py:117
  44.3 12.6 %copy-start.5 = (s32[4]{0:T(128)S(1)}, s32[4]{0:T(128)}, u32[]{:S(2)}) copy-start(s32[4]{0:T(128)} %param.13) | copy-start | bytes 52
  44.4 12.8 %copy-start.4 = (s32[1,4]{1,0:T(1,128)S(1)}, s32[1,4]{1,0:T(1,128)}, u32[]{:S(2)}) copy-start(s32[1,4]{1,0:T(1,128)} %param.17) | copy-start | bytes 52
  53.2 29.4 %all-to-all-start.1 = ((bf16[128,4,2048]{2,0,1:T(8,128)(2,1)}), bf16[128,4,2048]{2,0,1:T(8,128)(2,1)S(1)}, u32[]{:S(2)}, u32[]{:S(2)}) async-start(bf16[128,4,2048]{2,0,1:T(8,128)(2,1)} %bitcast.118), calls=%async_computation.1 | async-start | bytes 4194304 | tf_op jit(solution)/shard_map/all_to_all | solution.py:115
  82.6 18.3 %all-to-all-start.4 = ((bf16[8,32,512]{2,1,0:T(8,128)(2,1)}), bf16[8,32,512]{2,1,0:T(8,128)(2,1)S(1)}, u32[]{:S(2)}, u32[]{:S(2)}) async-start(bf16[8,32,512]{2,1,0:T(8,128)(2,1)} %copy.116), calls=%async_computation.4 | async-start | bytes 524288 | tf_op jit(solution)/shard_map/all_to_all | solution.py:153
  100.9 0.7 copy-start.3
  101.6 131.4 %all-to-all-start.7 = ((bf16[8,32,2048]{2,1,0:T(8,128)(2,1)}), bf16[8,32,2048]{2,1,0:T(8,128)(2,1)S(1)}, u32[]{:S(2)}, u32[]{:S(2)}) async-start(bf16[8,32,2048]{2,1,0:T(8,128)(2,1)} %copy.122), calls=%async_computation.7 | async-start | bytes 2097152 | tf_op jit(solution)/shard_map/all_to_all | solution.py:152
  116.5 2.2 copy-start
  123.1 2.0 copy-start.1
  129.3 2.2 copy-start
  135.8 2.0 copy-start.1
  142.0 2.2 copy-start
  148.5 2.0 copy-start.1
  154.7 2.2 copy-start
  161.2 2.0 copy-start.1
  167.4 2.2 copy-start
  173.9 2.0 copy-start.1
  180.1 2.2 copy-start
  186.6 2.0 copy-start.1
  192.8 2.2 copy-start
  199.3 2.0 copy-start.1
  205.5 2.2 copy-start
  212.0 2.0 copy-start.1
  233.0 29.9 %all-to-all-start.2 = ((bf16[4,128,2048]{2,1,0:T(8,128)(2,1)}), bf16[4,128,2048]{2,1,0:T(8,128)(2,1)S(1)}, u32[]{:S(2)}, u32[]{:S(2)}) async-start(bf16[4,128,2048]{2,1,0:T(8,128)(2,1)} %all_to_all.83), calls=%async_computation.2 | async-start | bytes 4194304 | tf_op jit(solution)/shard_map/all_to_all | solution.py:140
Sparse Core Ops, SparseCore 0:
  21.2 73.2 all-gather.1
where the time goes:
time: 278 us; the launch traced here: 276 us
  local copies, waits for them, and re-layouts  63.2 us (23%)
  matrix products  53.7 us (19%)
  waiting for transfers between devices  53.1 us (19%)
  other arithmetic  35.7 us (13%)
  starting transfers between devices  34.9 us (13%)
  between operations  14.2 us (5%)
  blocking collectives  11.4 us (4%)
  loops' own time  10 us (4%)
    dot_general x8, matrix products, update(): jnp.einsum('qhgk,khd->qhgd', weight.astype(jnp.bfloat16), key_value[:, :,...  35 us
    all_to_all x1, waiting for transfers between devices, per_device(): lax.all_to_all(long_q, 'head', split_axis=1, concat_axis=0, tiled=True)  24.3 us
    cond x40, local copies, waits for them, and re-layouts  16.5 us
    reduce_sum x8, other arithmetic, update(): denominator = denominator * factor + jnp.sum(weight, axis=-1)  16.4 us
    unnamed x15, local copies, waits for them, and re-layouts  16.1 us
    all_to_all x1, waiting for transfers between devices, per_device(): lax.all_to_all(long_att, 'head', split_axis=0, concat_axis=1, tiled=True)  13.4 us
    reduce_or x16, other arithmetic, block_step(): return lax.cond(jnp.any(visible), update, keep, attn_state)  13.3 us
    dot_general x8, matrix products, update(): jnp.einsum('qhgd,khd->qhgk', queries, key_value[:, :, 0], preferred_eleme...  13 us
  transfers between devices with their start and end apart: 8, of which 6 were waited for; matrix products, arithmetic and copies ran while one was open for 45% of the time, Pallas kernels for 0%

commit v1 on v0

v1 whole, which is shorter than its diff:
```python
import functools

import jax
import jax.numpy as jnp
from jax import lax
from jax.experimental import pallas as pl
from jax.experimental.pallas import tpu as pltpu
from jax.sharding import PartitionSpec as P

H = 64
KV = 8
HD = 128
SCAP = 32
LMAX = 2048
GROUP = H // KV
CHUNK = 128
BACK = 8
SLOTS = 2 * (BACK + 1)
WINDOW = SLOTS * CHUNK
LOG2E = 1.4426950408889634
EXP_SCALE = LOG2E * HD ** (-0.5)
masked_score = -1e30
MESH = pl.DeviceIdType.MESH
MIB = 1024 * 1024


def stacked_queries(q_ref, first_row, rows, first_head, heads):
    parts = [
        q_ref[first_row : first_row + rows, (first_head + g) * HD : (first_head + g + 1) * HD]
        for g in range(heads)
    ]
    return jnp.concatenate(parts, axis=0)


def attend(queries, keys, values, bias):
    scores = (
        lax.dot_general(
            queries, keys, (((1,), (1,)), ((), ())), preferred_element_type=jnp.float32
        )
        + bias
    )
    top = jnp.max(scores, axis=1, keepdims=True)
    weight = jnp.exp2((scores - top) * EXP_SCALE)
    total = jnp.sum(weight, axis=1, keepdims=True)
    out = jnp.dot(weight.astype(jnp.bfloat16), values, preferred_element_type=jnp.float32)
    return (out / total).astype(jnp.bfloat16)


def long_kernel(first_row_of, base_of, len_ref, q_ref, kv_ref, out_ref, bias_ref):
    rows = q_ref.shape[0]
    window = kv_ref.shape[0]

    @pl.when(pl.program_id(0) == 0)
    def _():
        query_pos = first_row_of() + lax.broadcasted_iota(jnp.int32, (rows, 1), 0)
        doc_start = jnp.zeros((rows, 1), jnp.int32)
        end = jnp.int32(0)
        for i in range(len_ref.shape[0]):
            end = end + len_ref[i]
            doc_start = jnp.where(query_pos >= end, end, doc_start)
        key_pos = base_of() + lax.broadcasted_iota(jnp.int32, (rows, window), 1)
        visible = (key_pos <= query_pos) & (key_pos >= doc_start)
        bias_ref[...] = jnp.where(visible, 0.0, masked_score)

    heads = 256 // rows
    keys = kv_ref[:, :HD]
    values = kv_ref[:, HD:]
    for block in range(GROUP // heads):
        first = block * heads
        queries = stacked_queries(q_ref, 0, rows, first, heads)
        bias = jnp.concatenate([bias_ref[...]] * heads, axis=0)
        out = attend(queries, keys, values, bias)
        for g in range(heads):
            out_ref[:, (first + g) * HD : (first + g + 1) * HD] = out[g * rows : (g + 1) * rows]


def long_attention(first_row_of, base_of, lengths, q, window):
    rows, keys = q.shape[0], window.shape[0]
    scores = H * rows * keys
    return pl.pallas_call(
        functools.partial(long_kernel, first_row_of, base_of),
        grid=(KV,),
        out_shape=jax.ShapeDtypeStruct(q.shape, jnp.bfloat16),
        in_specs=[
            pl.BlockSpec(memory_space=pltpu.SMEM),
            pl.BlockSpec((rows, GROUP * HD), lambda h: (0, h)),
            pl.BlockSpec((keys, 2 * HD), lambda h: (0, h)),
        ],
        out_specs=pl.BlockSpec((rows, GROUP * HD), lambda h: (0, h)),
        scratch_shapes=[pltpu.VMEM((rows, keys), jnp.float32)],
        compiler_params=pltpu.CompilerParams(vmem_limit_bytes=50 * MIB),
        cost_estimate=pl.CostEstimate(
            flops=4 * HD * scores, bytes_accessed=4 * q.size + 2 * window.size, transcendentals=scores
        ),
    )(lengths, q, window)


def short_kernel(q_ref, kv_ref, docs_ref, out_ref):
    groups = q_ref.shape[0] // SCAP
    first_group = lax.axis_index("head") * groups
    row = lax.broadcasted_iota(jnp.int32, (SCAP, SCAP), 0)
    col = lax.broadcasted_iota(jnp.int32, (SCAP, SCAP), 1)
    for j in range(groups):
        key_doc = jnp.broadcast_to(docs_ref[pl.ds(first_group + j, 1), :], (SCAP, SCAP))
        query_doc = jnp.sum(jnp.where(row == col, key_doc, 0), axis=1, keepdims=True)
        visible = (key_doc == query_doc) & (col <= row)
        bias = jnp.concatenate([jnp.where(visible, 0.0, masked_score)] * GROUP, axis=0)
        rows = slice(j * SCAP, (j + 1) * SCAP)
        for h in range(KV):
            out = attend(
                stacked_queries(q_ref, j * SCAP, SCAP, h * GROUP, GROUP),
                kv_ref[rows, 2 * h * HD : (2 * h + 1) * HD],
                kv_ref[rows, (2 * h + 1) * HD : (2 * h + 2) * HD],
                bias,
            )
            for g in range(GROUP):
                head = h * GROUP + g
                out_ref[rows, head * HD : (head + 1) * HD] = out[g * SCAP : (g + 1) * SCAP]


def short_attention(q, kv, docs):
    return pl.pallas_call(
        short_kernel,
        out_shape=jax.ShapeDtypeStruct(q.shape, jnp.bfloat16),
        in_specs=[pl.BlockSpec(memory_space=pltpu.VMEM)] * 3,
        out_specs=pl.BlockSpec(memory_space=pltpu.VMEM),
        compiler_params=pltpu.CompilerParams(vmem_limit_bytes=32 * MIB),
    )(q, kv, docs)


X0, X1, X2, Y0, Y1, Y2, Z1, Z2, D0, D1, D2, OWN = range(12)


def exchange_kernel(
    kv_ref, att_ref, dest_ref, win_ref, short_ref,
    gathered, outgoing,
    send_sem, recv_sem, pair_send, pair_recv, head_send, head_recv, ctx_send, ctx_recv,
    local_sem, fill_sem,
):
    ctx, head = lax.axis_index("ctx"), lax.axis_index("head")
    ctx_count, head_count = lax.axis_size("ctx"), lax.axis_size("head")
    z, y, x, c = ctx // 2, ctx % 2, head // 2, head % 2
    chip = ctx * 2 + x
    cols = gathered.shape[2]

    barrier = pltpu.get_barrier_semaphore()
    for k in range(1, head_count):
        pl.semaphore_signal(
            barrier, inc=1, device_id=(ctx, (head + k) % head_count), device_id_type=MESH
        )
    for k in range(1, ctx_count):
        pl.semaphore_signal(
            barrier, inc=1, device_id=((ctx + k) % ctx_count, head), device_id_type=MESH
        )
    pl.semaphore_wait(barrier, head_count + ctx_count - 2)

    def slot(back):
        return (BACK - back) * 2 + c

    x_peer = (ctx, (1 - x) * 2 + c)
    y_peer = (z * 2 + 1 - y, head)
    z_next = ((ctx + 2) % ctx_count, head)
    sibling = (ctx, x * 2 + 1 - c)
    x_step = 1 - 2 * x
    y_step = 2 - 4 * y

    def link(event, src, back, device):
        return pltpu.make_async_remote_copy(
            src_ref=src, dst_ref=win_ref.at[slot(back)], send_sem=send_sem.at[event],
            recv_sem=recv_sem.at[event], device_id=device, device_id_type=MESH,
        )

    def held(back):
        return win_ref.at[slot(back)]

    last_z = z >= ctx_count // 2 - 1
    sends = {
        Z1: (~last_z, lambda: link(Z1, kv_ref, 4, z_next)),
        X0: (x == 0, lambda: link(X0, kv_ref, 1, x_peer)),
        Y0: (y == 0, lambda: link(Y0, kv_ref, 2, y_peer)),
        Z2: ((z >= 1) & ~last_z, lambda: link(Z2, held(4), 8, z_next)),
        X1: (z >= 1, lambda: link(X1, held(4), 4 + x_step, x_peer)),
        Y1: (z >= 1, lambda: link(Y1, held(4), 4 + y_step, y_peer)),
        X2: ((z >= 2) & (x == 1), lambda: link(X2, held(8), 7, x_peer)),
        Y2: ((z >= 2) & (y == 1), lambda: link(Y2, held(8), 6, y_peer)),
        D0: (y == 1, lambda: link(D0, held(2), 2 + x_step, x_peer)),
        D1: (z >= 1, lambda: link(D1, held(4 - x_step), 4 - x_step + y_step, y_peer)),
        D2: ((z >= 2) & (y == 0), lambda: link(D2, held(6), 6 + x_step, x_peer)),
    }
    arrivals = {
        X0: (x == 1, 1),
        X1: (z >= 1, 4 - x_step),
        X2: ((z >= 2) & (x == 0), 7),
        Y0: (y == 1, 2),
        Y1: (z >= 1, 4 - y_step),
        Y2: ((z >= 2) & (y == 0), 6),
        Z1: (z >= 1, 4),
        Z2: (z >= 2, 8),
        D0: (y == 1, 2 - x_step),
        D1: (z >= 1, 4 - x_step - y_step),
        D2: ((z >= 2) & (y == 0), 6 - x_step),
    }

    def pair(event):
        back = 0 if event == OWN else arrivals[event][1]
        src = kv_ref if event == OWN else held(back)
        return pltpu.make_async_remote_copy(
            src_ref=src, dst_ref=held(back), send_sem=pair_send.at[event],
            recv_sem=pair_recv.at[event], device_id=sibling, device_id_type=MESH,
        )

    def start(event):
        condition, make = sends[event]

        @pl.when(condition)
        def _():
            make().start()

    def arrive(event, *then):
        condition, back = arrivals[event]

        @pl.when(condition)
        def _():
            link(event, kv_ref, back, sibling).wait_recv()
            for other in then:
                start(other)
            pair(event).start()

    def head_copy(k):
        peer = (head + k) % head_count
        return pltpu.make_async_remote_copy(
            src_ref=att_ref.at[:, pl.ds(pl.multiple_of(peer * cols, cols), cols)],
            dst_ref=gathered.at[head], send_sem=head_send.at[k], recv_sem=head_recv.at[k],
            device_id=(ctx, peer), device_id_type=MESH,
        )

    def ctx_copy(k):
        peer = (ctx + k) % ctx_count
        return pltpu.make_async_remote_copy(
            src_ref=outgoing.at[peer], dst_ref=short_ref.at[ctx], send_sem=ctx_send.at[k],
            recv_sem=ctx_recv.at[k], device_id=(peer, head), device_id_type=MESH,
        )

    for k in range(1, head_count):
        head_copy(k).start()
    own_att = pltpu.make_async_copy(
        att_ref.at[:, pl.ds(pl.multiple_of(head * cols, cols), cols)], gathered.at[head],
        local_sem.at[0],
    )
    own_att.start()
    for event in (Z1, X0, Y0):
        start(event)
    pair(OWN).start()
    own_kv = pltpu.make_async_copy(kv_ref, held(0), local_sem.at[1])
    own_kv.start()

    def fill(index):
        return pltpu.make_async_copy(kv_ref, win_ref.at[index], fill_sem.at[index])

    for index in range(2 * BACK):

        @pl.when(chip < BACK - index // 2)
        def _(index=index):
            fill(index).start()

    own_att.wait()
    for k in range(1, head_count):
        head_copy(k).wait_recv()
    for e in range(ctx_count):
        placed = jnp.zeros(gathered.shape[1:], gathered.dtype)
        for g in range(head_count):
            placed = jnp.where(dest_ref[0, g] == e, gathered[g], placed)
        outgoing[e] = placed
    for k in range(1, ctx_count):
        ctx_copy(k).start()
    own_short = pltpu.make_async_copy(outgoing.at[ctx], short_ref.at[ctx], local_sem.at[2])
    own_short.start()

    arrive(Y0, D0)
    arrive(X0)
    arrive(Z1, Z2, X1, Y1)
    arrive(Z2, X2, Y2)
    arrive(X1, D1)
    arrive(Y2, D2)
    for event in (Y1, X2, D0, D1, D2):
        arrive(event)

    pair(OWN).wait()
    for event in range(OWN):

        @pl.when(sends[event][0])
        def _(event=event):
            sends[event][1]().wait_send()

        @pl.when(arrivals[event][0])
        def _(event=event):
            pair(event).wait()

    own_kv.wait()
    own_short.wait()
    for index in range(2 * BACK):

        @pl.when(chip < BACK - index // 2)
        def _(index=index):
            fill(index).wait()

    for k in range(1, head_count):
        head_copy(k).wait_send()
    for k in range(1, ctx_count):
        ctx_copy(k).wait()


def exchange(kv, att, dest):
    ctx_count, head_count = lax.axis_size("ctx"), lax.axis_size("head")
    cols = att.shape[1] // head_count
    dma = pltpu.SemaphoreType.DMA
    return pl.pallas_call(
        exchange_kernel,
        out_shape=(
            jax.ShapeDtypeStruct((SLOTS, CHUNK, kv.shape[1]), jnp.bfloat16),
            jax.ShapeDtypeStruct((ctx_count, SCAP, cols), jnp.bfloat16),
        ),
        in_specs=[
            pl.BlockSpec(memory_space=pl.ANY),
            pl.BlockSpec(memory_space=pl.ANY),
            pl.BlockSpec(memory_space=pltpu.SMEM),
        ],
        out_specs=(pl.BlockSpec(memory_space=pl.ANY), pl.BlockSpec(memory_space=pl.ANY)),
        scratch_shapes=[
            pltpu.VMEM((head_count, SCAP, cols), jnp.bfloat16),
            pltpu.VMEM((ctx_count, SCAP, cols), jnp.bfloat16),
            dma((12,)), dma((12,)), dma((12,)), dma((12,)),
            dma((head_count,)), dma((head_count,)), dma((ctx_count,)), dma((ctx_count,)),
            dma((3,)), dma((2 * BACK,)),
        ],
        compiler_params=pltpu.CompilerParams(
            collective_id=0, has_side_effects=True, vmem_limit_bytes=16 * MIB
        ),
        cost_estimate=pl.CostEstimate(flops=0, bytes_accessed=40 * MIB, transcendentals=0),
    )(kv, att, dest)


def place_groups(dest, rows_array, groups, ctx_count):
    shaped = rows_array.reshape(groups, SCAP, rows_array.shape[1])
    hit = dest[None, :] == jnp.arange(ctx_count, dtype=jnp.int32)[:, None]
    which = jnp.argmax(hit, axis=1)
    return jnp.where(jnp.any(hit, axis=1)[:, None, None], shaped[which], 0)


def per_device(long_q, long_kv, long_lengths, short_q, short_kv, short_docs, short_dest):
    ctx_count, head_count = lax.axis_size("ctx"), lax.axis_size("head")
    rows = long_q.shape[0]

    def rank():
        return lax.axis_index("ctx") * head_count + lax.axis_index("head")

    def first_row_of():
        return rank() * rows

    short_att = short_attention(short_q, short_kv, short_docs)
    if ctx_count == 8 and head_count == 4 and rows == CHUNK and short_q.shape[0] == SCAP:

        def base_of():
            return (rank() // 2 - BACK) * 2 * CHUNK

        window, short_out = exchange(long_kv, short_att, short_dest)
        window = window.reshape(WINDOW, long_kv.shape[1])
        short_out = short_out.reshape(ctx_count * SCAP, -1)
    else:

        def base_of():
            return jnp.maximum(first_row_of() + rows - WINDOW, 0)

        everything = lax.all_gather(long_kv, ("ctx", "head"), axis=0, tiled=True)
        window = lax.dynamic_slice_in_dim(everything, base_of(), WINDOW, 0)
        gathered = lax.all_to_all(short_att, "head", split_axis=1, concat_axis=0, tiled=True)
        placed = place_groups(short_dest[0], gathered, short_dest.shape[1], ctx_count)
        arrived = lax.all_to_all(placed, "ctx", split_axis=0, concat_axis=0, tiled=True)
        short_out = arrived.reshape(ctx_count * SCAP, -1)
    long_out = long_attention(first_row_of, base_of, long_lengths, long_q, window)
    return (long_out, short_out)


def solution(mesh):
    in_specs = (
        P(("ctx", "head"), None),
        P(("ctx", "head"), None),
        P(),
        P(("ctx", "head"), None),
        P(("ctx", "head"), None),
        P("ctx", None),
        P("ctx", None),
    )
    out_specs = (P(("ctx", "head"), None), P("ctx", "head"))
    return jax.shard_map(
        per_device, mesh=mesh, in_specs=in_specs, out_specs=out_specs, check_vma=False
    )
```

time: 278 us -> 123 us (0.44)
  the two profiles are of different devices: /device:TPU:12 before, /device:TPU:17 now
where the time goes in v1:
time: 123 us
  Pallas kernels  112 us (91%)
  local copies, waits for them, and re-layouts  10.5 us (9%)
    pallas_call x1, Pallas kernels, exchange(): pl.pallas_call(exchange_kernel, out_shape=(jax.ShapeDtypeStruct((SLOTS, C...  76.7 us
    pallas_call x1, Pallas kernels, long_attention(): pl.pallas_call(functools.partial(long_kernel, first_row_of, base_of), gri...  34.3 us
    unnamed x17, local copies, waits for them, and re-layouts  10.5 us

profile of v1, /device:TPU:17, one launch (start us, length us, event | category | flops | bytes accessed | tf_op | source)
XLA Modules:
  0.0 123.0 jit_solution(17181564936492635896)
XLA Ops:
  0.6 0.0 copy-start
  0.6 1.0 copy-done
  1.7 0.0 copy-start.2
  1.7 0.9 copy-done.2
  2.6 0.0 copy-start.3
  2.6 0.7 copy-done.3
  3.3 0.0 copy-start.7
  3.3 0.9 shard_map.86.att_ref
  4.2 0.0 copy-start.1
  4.2 1.0 copy-done.1
  5.2 0.0 copy-start.4
  5.2 0.7 copy-done.4
  5.9 76.7 %shard_map.87 = (bf16[18,128,2048]{2,1,0:T(8,128)(2,1)S(1)}, bf16[8,32,2048]{2,1,0:T(8,128)(2,1)S(1)}) custom-call(bf16[128,2048]{1,0:T(8,128)(2,1)S(1)} %copy-done.1, bf16[32,8192]{1,0:T(8,128)(2,1)S(1)} %shard_map.86.att_ref, s32[1,4]{1,0:T(1,128)S(1)} %copy-done.4), custom_call_target="tpu_custom_call" | custom-call | bytes 41943040 | tf_op jit(solution)/shard_map/pallas_call | solution.py:317
  82.6 0.0 copy-start.5
  82.6 3.6 %copy-done.5 = bf16[18,128,2048]{2,1,0:T(8,128)(2,1)} copy-done((bf16[18,128,2048]{2,1,0:T(8,128)(2,1)}, bf16[18,128,2048]{2,1,0:T(8,128)(2,1)S(1)}, u32[]{:S(2)}) %copy-start.5) | copy-done | bytes 9437208
  86.2 0.0 copy-done.7
  86.2 0.0 copy-start.6
  86.2 1.6 %copy-done.6 = bf16[128,8192]{1,0:T(8,128)(2,1)S(1)} copy-done((bf16[128,8192]{1,0:T(8,128)(2,1)S(1)}, bf16[128,8192]{1,0:T(8,128)(2,1)}, u32[]{:S(2)}) %copy-start.6) | copy-done | bytes 2097176
  87.8 34.3 %shard_map.88 = bf16[128,8192]{1,0:T(8,128)(2,1)} custom-call(s32[4]{0:T(128)S(1)} %copy-done.7, bf16[128,8192]{1,0:T(8,128)(2,1)S(1)} %copy-done.6, bf16[2304,2048]{1,0:T(8,128)(2,1)} %bitcast.3), custom_call_target="tpu_custom_call" | custom-call | flops 9663676416 | bytes 13631488 | tf_op jit(solution)/shard_map/pallas_call | solution.py:80
  122.1 1.0 copy.10
Async XLA Ops:
  0.6 1.0 copy-start
  1.7 0.9 copy-start.2
  2.6 0.7 copy-start.3
  3.3 83.0 %copy-start.7 = (s32[4]{0:T(128)S(1)}, s32[4]{0:T(128)}, u32[]{:S(2)}) copy-start(s32[4]{0:T(128)} %len_ref.1) | copy-start | bytes 52
  4.2 1.0 copy-start.1
  5.2 0.7 copy-start.4
  82.6 3.6 %copy-start.5 = (bf16[18,128,2048]{2,1,0:T(8,128)(2,1)}, bf16[18,128,2048]{2,1,0:T(8,128)(2,1)S(1)}, u32[]{:S(2)}) copy-start(bf16[18,128,2048]{2,1,0:T(8,128)(2,1)S(1)} %get-tuple-element.4) | copy-start | bytes 28311556
  86.2 1.6 %copy-start.6 = (bf16[128,8192]{1,0:T(8,128)(2,1)S(1)}, bf16[128,8192]{1,0:T(8,128)(2,1)}, u32[]{:S(2)}) copy-start(bf16[128,8192]{1,0:T(8,128)(2,1)} %q_ref.3) | copy-start | bytes 6291460

commit v2 on v1

--- a/solution.py
+++ b/solution.py
@@ -15,8 +15,13 @@
 GROUP = H // KV
 CHUNK = 128
 BACK = 8
+PIECES = 4
+PART = CHUNK // PIECES
+HEADS = 2
 SLOTS = 2 * (BACK + 1)
 WINDOW = SLOTS * CHUNK
+FAR = BACK
+NEAR = SLOTS - FAR
 LOG2E = 1.4426950408889634
 EXP_SCALE = LOG2E * HD ** (-0.5)
 masked_score = -1e30
@@ -132,8 +137,8 @@
 
 
 def exchange_kernel(
-    kv_ref, att_ref, dest_ref, win_ref, short_ref,
-    gathered, outgoing,
+    len_ref, dest_ref, q_ref, kv_ref, att_ref, long_ref, short_ref,
+    win_ref, acc_ref, top_ref, total_ref, start_ref, bias_ref, gathered, outgoing,
     send_sem, recv_sem, pair_send, pair_recv, head_send, head_recv, ctx_send, ctx_recv,
     local_sem, fill_sem,
 ):
@@ -164,10 +169,14 @@
     x_step = 1 - 2 * x
     y_step = 2 - 4 * y
 
-    def link(event, src, back, device):
+    def part(ref, p):
+        return ref.at[pl.ds(p * PART, PART)]
+
+    def link(event, p, src, back, device):
         return pltpu.make_async_remote_copy(
-            src_ref=src, dst_ref=win_ref.at[slot(back)], send_sem=send_sem.at[event],
-            recv_sem=recv_sem.at[event], device_id=device, device_id_type=MESH,
+            src_ref=part(src, p), dst_ref=part(win_ref.at[slot(back)], p),
+            send_sem=send_sem.at[event, p], recv_sem=recv_sem.at[event, p],
+            device_id=device, device_id_type=MESH,
         )
 
     def held(back):
@@ -175,17 +184,17 @@
 
     last_z = z >= ctx_count // 2 - 1
     sends = {
-        Z1: (~last_z, lambda: link(Z1, kv_ref, 4, z_next)),
-        X0: (x == 0, lambda: link(X0, kv_ref, 1, x_peer)),
-        Y0: (y == 0, lambda: link(Y0, kv_ref, 2, y_peer)),
-        Z2: ((z >= 1) & ~last_z, lambda: link(Z2, held(4), 8, z_next)),
-        X1: (z >= 1, lambda: link(X1, held(4), 4 + x_step, x_peer)),
-        Y1: (z >= 1, lambda: link(Y1, held(4), 4 + y_step, y_peer)),
-        X2: ((z >= 2) & (x == 1), lambda: link(X2, held(8), 7, x_peer)),
-        Y2: ((z >= 2) & (y == 1), lambda: link(Y2, held(8), 6, y_peer)),
-        D0: (y == 1, lambda: link(D0, held(2), 2 + x_step, x_peer)),
-        D1: (z >= 1, lambda: link(D1, held(4 - x_step), 4 - x_step + y_step, y_peer)),
-        D2: ((z >= 2) & (y == 0), lambda: link(D2, held(6), 6 + x_step, x_peer)),
+        Z1: (~last_z, lambda p: link(Z1, p, kv_ref, 4, z_next)),
+        X0: (x == 0, lambda p: link(X0, p, kv_ref, 1, x_peer)),
+        Y0: (y == 0, lambda p: link(Y0, p, kv_ref, 2, y_peer)),
+        Z2: ((z >= 1) & ~last_z, lambda p: link(Z2, p, held(4), 8, z_next)),
+        X1: (z >= 1, lambda p: link(X1, p, held(4), 4 + x_step, x_peer)),
+        Y1: (z >= 1, lambda p: link(Y1, p, held(4), 4 + y_step, y_peer)),
+        X2: ((z >= 2) & (x == 1), lambda p: link(X2, p, held(8), 7, x_peer)),
+        Y2: ((z >= 2) & (y == 1), lambda p: link(Y2, p, held(8), 6, y_peer)),
+        D0: (y == 1, lambda p: link(D0, p, held(2), 2 + x_step, x_peer)),
+        D1: (z >= 1, lambda p: link(D1, p, held(4 - x_step), 4 - x_step + y_step, y_peer)),
+        D2: ((z >= 2) & (y == 0), lambda p: link(D2, p, held(6), 6 + x_step, x_peer)),
     }
     arrivals = {
         X0: (x == 1, 1),
@@ -201,30 +210,124 @@
         D2: ((z >= 2) & (y == 0), 6 - x_step),
     }
 
-    def pair(event):
+    def pair(event, p):
         back = 0 if event == OWN else arrivals[event][1]
         src = kv_ref if event == OWN else held(back)
         return pltpu.make_async_remote_copy(
-            src_ref=src, dst_ref=held(back), send_sem=pair_send.at[event],
-            recv_sem=pair_recv.at[event], device_id=sibling, device_id_type=MESH,
-        )
-
-    def start(event):
+            src_ref=part(src, p), dst_ref=part(held(back), p), send_sem=pair_send.at[event, p],
+            recv_sem=pair_recv.at[event, p], device_id=sibling, device_id_type=MESH,
+        )
+
+    def start(event, p):
         condition, make = sends[event]
 
         @pl.when(condition)
         def _():
-            make().start()
-
-    def arrive(event, *then):
+            make(p).start()
+
+    def arrive(p, event, *then):
         condition, back = arrivals[event]
 
         @pl.when(condition)
         def _():
-            link(event, kv_ref, back, sibling).wait_recv()
+            link(event, p, kv_ref, back, sibling).wait_recv()
             for other in then:
-                start(other)
-            pair(event).start()
+                start(other, p)
+            pair(event, p).start()
+
+    first_row = (ctx * head_count + head) * CHUNK
+
+    def find_starts():
+        query_pos = first_row + lax.broadcasted_iota(jnp.int32, (CHUNK, HD), 0)
+        doc_start = jnp.zeros((CHUNK, HD), jnp.int32)
+        end = jnp.int32(0)
+        for i in range(len_ref.shape[0]):
+            end = end + len_ref[i]
+            doc_start = jnp.where(query_pos >= end, end, doc_start)
+        start_ref[...] = doc_start
+
+    def set_bias(first_slot, slots):
+        query_pos = first_row + lax.broadcasted_iota(jnp.int32, (CHUNK, HD), 0)
+        for index in range(slots):
+            key_pos = (
+                (chip - BACK) * 2 * CHUNK
+                + (first_slot + index) * CHUNK
+                + lax.broadcasted_iota(jnp.int32, (CHUNK, HD), 1)
+            )
+            visible = (key_pos <= query_pos) & (key_pos >= start_ref[...])
+            bias_ref[:, index * CHUNK : (index + 1) * CHUNK] = jnp.where(
+                visible, 0.0, masked_score
+            )
+
+    def attend_slots(first_slot, slots, merge, from_head, to_head):
+        def one(h, carry):
+            key_cols = pl.ds(pl.multiple_of(h * 2 * HD, HD), HD)
+            value_cols = pl.ds(pl.multiple_of((h * 2 + 1) * HD, HD), HD)
+            which = pl.ds(first_slot, slots)
+            keys = win_ref[which, :, key_cols].reshape(slots * CHUNK, HD)
+            values = win_ref[which, :, value_cols].reshape(slots * CHUNK, HD)
+            for block in range(GROUP // HEADS):
+                first_head = h * GROUP + block * HEADS
+                queries = jnp.concatenate(
+                    [
+                        q_ref[:, pl.ds(pl.multiple_of((first_head + g) * HD, HD), HD)]
+                        for g in range(HEADS)
+                    ],
+                    axis=0,
+                )
+                bias = jnp.concatenate([bias_ref[:, : slots * CHUNK]] * HEADS, axis=0)
+                scores = (
+                    lax.dot_general(
+                        queries, keys, (((1,), (1,)), ((), ())), preferred_element_type=jnp.float32
+                    )
+                    + bias
+                )
+                rows = pl.ds(block * HEADS * CHUNK, HEADS * CHUNK)
+                shape = (HEADS * CHUNK, HD)
+                top = jnp.max(scores, axis=1, keepdims=True)
+                weight = jnp.exp2((scores - top) * EXP_SCALE)
+                total = jnp.sum(weight, axis=1, keepdims=True)
+                numerator = jnp.dot(
+                    weight.astype(jnp.bfloat16), values, preferred_element_type=jnp.float32
+                )
+                top = jnp.broadcast_to(top, shape)
+                total = jnp.broadcast_to(total, shape)
+                if not merge:
+                    top_ref[h, rows, :] = top
+                    total_ref[h, rows, :] = total
+                    acc_ref[h, rows, :] = numerator
+                else:
+                    before = top_ref[h, rows, :]
+                    both = jnp.maximum(before, top)
+                    factor = jnp.exp2((before - both) * EXP_SCALE)
+                    scale = jnp.exp2((top - both) * EXP_SCALE)
+                    total = total_ref[h, rows, :] * factor + total * scale
+                    numerator = acc_ref[h, rows, :] * factor + numerator * scale
+                    out = (numerator / total).astype(jnp.bfloat16)
+                    for g in range(HEADS):
+                        cols_of = pl.ds(pl.multiple_of((first_head + g) * HD, HD), HD)
+                        long_ref[:, cols_of] = out[g * CHUNK : (g + 1) * CHUNK]
+            return carry
+
+        lax.fori_loop(from_head, to_head, one, 0)
+
+    def ready(event):
+        @pl.when(arrivals[event][0])
+        def _():
+            for p in range(PIECES):
+                pair(event, p).wait_recv()
+
+    def finish():
+        def one(h, carry):
+            for g in range(GROUP):
+                rows = pl.ds(g * CHUNK, CHUNK)
+                cols_of = pl.ds(pl.multiple_of((h * GROUP + g) * HD, HD), HD)
+                long_ref[:, cols_of] = (acc_ref[h, rows, :] / total_ref[h, rows, :]).astype(
+                    jnp.bfloat16
+                )
+            return carry
+
+        lax.fori_loop(0, KV, one, 0)
 
     def head_copy(k):
         peer = (head + k) % head_count
@@ -248,9 +351,11 @@
         local_sem.at[0],
     )
     own_att.start()
-    for event in (Z1, X0, Y0):
-        start(event)
-    pair(OWN).start()
+    for p in range(PIECES):
+        for event in (Z1, X0, Y0):
+            start(event, p)
+    for p in range(PIECES):
+        pair(OWN, p).start()
     own_kv = pltpu.make_async_copy(kv_ref, held(0), local_sem.at[1])
     own_kv.start()
 
@@ -262,6 +367,16 @@
         @pl.when(chip < BACK - index // 2)
         def _(index=index):
             fill(index).start()
+
+    find_starts()
+    set_bias(FAR, NEAR)
+    for p in range(PIECES):
+        arrive(p, Z1, Z2, X1, Y1)
+        arrive(p, Y0, D0)
+        arrive(p, X0)
+    for p in range(PIECES):
+        arrive(p, Z2, X2, Y2)
+        arrive(p, X1, D1)
 
     own_att.wait()
     for k in range(1, head_count):
@@ -271,73 +386,102 @@
         for g in range(head_count):
             placed = jnp.where(dest_ref[0, g] == e, gathered[g], placed)
         outgoing[e] = placed
-    for k in range(1, ctx_count):
-        ctx_copy(k).start()
     own_short = pltpu.make_async_copy(outgoing.at[ctx], short_ref.at[ctx], local_sem.at[2])
     own_short.start()
 
-    arrive(Y0, D0)
-    arrive(X0)
-    arrive(Z1, Z2, X1, Y1)
-    arrive(Z2, X2, Y2)
-    arrive(X1, D1)
-    arrive(Y2, D2)
-    for event in (Y1, X2, D0, D1, D2):
-        arrive(event)
-
-    pair(OWN).wait()
-    for event in range(OWN):
-
-        @pl.when(sends[event][0])
-        def _(event=event):
-            sends[event][1]().wait_send()
-
-        @pl.when(arrivals[event][0])
-        def _(event=event):
-            pair(event).wait()
-
-    own_kv.wait()
-    own_short.wait()
+    for event in (Y1, D0, D1):
+        for p in range(PIECES):
+            arrive(p, event)
     for index in range(2 * BACK):
 
         @pl.when(chip < BACK - index // 2)
         def _(index=index):
             fill(index).wait()
 
+    own_kv.wait()
+    for p in range(PIECES):
+        pair(OWN, p).wait_recv()
+    for event in (X0, Y0, Z1, X1, Y1, D0, D1):
+        ready(event)
+    for k in range(1, ctx_count):
+        ctx_copy(k).start()
+    for p in range(PIECES):
+        attend_slots(FAR, NEAR, False, p, p + 1)
+        arrive(p, Y2, D2)
+    for p in range(PIECES):
+        arrive(p, X2)
+    attend_slots(FAR, NEAR, False, KV // 2, KV)
+    for p in range(PIECES):
+        arrive(p, D2)
+    for event in (Z2, X2, Y2, D2):
+        ready(event)
+
+    @pl.when(chip > BACK // 2)
+    def _():
+        set_bias(0, FAR)
+        attend_slots(0, FAR, True, 0, KV)
+
+    @pl.when(chip <= BACK // 2)
+    def _():
+        finish()
+
+    for p in range(PIECES):
+        pair(OWN, p).wait_send()
+        for event in range(OWN):
+
+            @pl.when(sends[event][0])
+            def _(event=event, p=p):
+                sends[event][1](p).wait_send()
+
+            @pl.when(arrivals[event][0])
+            def _(event=event, p=p):
+                pair(event, p).wait_send()
+
+    own_short.wait()
     for k in range(1, head_count):
         head_copy(k).wait_send()
     for k in range(1, ctx_count):
         ctx_copy(k).wait()
 
 
-def exchange(kv, att, dest):
+def exchange(lengths, dest, q, kv, att):
     ctx_count, head_count = lax.axis_size("ctx"), lax.axis_size("head")
     cols = att.shape[1] // head_count
     dma = pltpu.SemaphoreType.DMA
+    scores = H * CHUNK * WINDOW
+    state = pltpu.VMEM((KV, GROUP * CHUNK, HD), jnp.float32)
     return pl.pallas_call(
         exchange_kernel,
         out_shape=(
-            jax.ShapeDtypeStruct((SLOTS, CHUNK, kv.shape[1]), jnp.bfloat16),
+            jax.ShapeDtypeStruct(q.shape, jnp.bfloat16),
             jax.ShapeDtypeStruct((ctx_count, SCAP, cols), jnp.bfloat16),
         ),
         in_specs=[
+            pl.BlockSpec(memory_space=pltpu.SMEM),
+            pl.BlockSpec(memory_space=pltpu.SMEM),
+            pl.BlockSpec(memory_space=pltpu.VMEM),
             pl.BlockSpec(memory_space=pl.ANY),
             pl.BlockSpec(memory_space=pl.ANY),
-            pl.BlockSpec(memory_space=pltpu.SMEM),
         ],
-        out_specs=(pl.BlockSpec(memory_space=pl.ANY), pl.BlockSpec(memory_space=pl.ANY)),
+        out_specs=(pl.BlockSpec(memory_space=pltpu.VMEM), pl.BlockSpec(memory_space=pl.ANY)),
         scratch_shapes=[
+            pltpu.VMEM((SLOTS, CHUNK, kv.shape[1]), jnp.bfloat16),
+            state, state, state,
+            pltpu.VMEM((CHUNK, HD), jnp.int32),
+            pltpu.VMEM((CHUNK, NEAR * CHUNK), jnp.float32),
             pltpu.VMEM((head_count, SCAP, cols), jnp.bfloat16),
             pltpu.VMEM((ctx_count, SCAP, cols), jnp.bfloat16),
-            dma((12,)), dma((12,)), dma((12,)), dma((12,)),
+            dma((12, PIECES)), dma((12, PIECES)), dma((12, PIECES)), dma((12, PIECES)),
             dma((head_count,)), dma((head_count,)), dma((ctx_count,)), dma((ctx_count,)),
             dma((3,)), dma((2 * BACK,)),
         ],
         compiler_params=pltpu.CompilerParams(
-            collective_id=0, has_side_effects=True, vmem_limit_bytes=16 * MIB
+            collective_id=0, has_side_effects=True, vmem_limit_bytes=50 * MIB
         ),
-        cost_estimate=pl.CostEstimate(flops=0, bytes_accessed=40 * MIB, transcendentals=0),
-    )(kv, att, dest)
+        cost_estimate=pl.CostEstimate(
+            flops=4 * HD * scores, bytes_accessed=16 * MIB, transcendentals=scores
+        ),
+    )(lengths, dest, q, kv, att)
 
 
 def place_groups(dest, rows_array, groups, ctx_count):
@@ -359,24 +503,18 @@
 
     short_att = short_attention(short_q, short_kv, short_docs)
     if ctx_count == 8 and head_count == 4 and rows == CHUNK and short_q.shape[0] == SCAP:
-
-        def base_of():
-            return (rank() // 2 - BACK) * 2 * CHUNK
-
-        window, short_out = exchange(long_kv, short_att, short_dest)
-        window = window.reshape(WINDOW, long_kv.shape[1])
-        short_out = short_out.reshape(ctx_count * SCAP, -1)
-    else:
-
-        def base_of():
-            return jnp.maximum(first_row_of() + rows - WINDOW, 0)
-
-        everything = lax.all_gather(long_kv, ("ctx", "head"), axis=0, tiled=True)
-        window = lax.dynamic_slice_in_dim(everything, base_of(), WINDOW, 0)
-        gathered = lax.all_to_all(short_att, "head", split_axis=1, concat_axis=0, tiled=True)
-        placed = place_groups(short_dest[0], gathered, short_dest.shape[1], ctx_count)
-        arrived = lax.all_to_all(placed, "ctx", split_axis=0, concat_axis=0, tiled=True)
-        short_out = arrived.reshape(ctx_count * SCAP, -1)
+        long_out, short_out = exchange(long_lengths, short_dest, long_q, long_kv, short_att)
+        return (long_out, short_out.reshape(ctx_count * SCAP, -1))
+
+    def base_of():
+        return jnp.maximum(first_row_of() + rows - WINDOW, 0)
+
+    everything = lax.all_gather(long_kv, ("ctx", "head"), axis=0, tiled=True)
+    window = lax.dynamic_slice_in_dim(everything, base_of(), WINDOW, 0)
+    gathered = lax.all_to_all(short_att, "head", split_axis=1, concat_axis=0, tiled=True)
+    placed = place_groups(short_dest[0], gathered, short_dest.shape[1], ctx_count)
+    arrived = lax.all_to_all(placed, "ctx", split_axis=0, concat_axis=0, tiled=True)
+    short_out = arrived.reshape(ctx_count * SCAP, -1)
     long_out = long_attention(first_row_of, base_of, long_lengths, long_q, window)
     return (long_out, short_out)
 

time: 123 us -> 104 us (0.85)
  Pallas kernels: 112 us -> 93.6 us
  local copies, waits for them, and re-layouts: 10.5 us -> 9.03 us
    pallas_call x2 -> x1, Pallas kernels: 111 us -> 92.7 us  [exchange(): pl.pallas_call(exchange_kernel, out_shape=(jax.ShapeDtypeStruct(q.shape,...]
    unnamed x17 -> x14, local copies, waits for them, and re-layouts: 10.5 us -> 9.03 us
where the time goes in v2:
time: 104 us; the launch traced here: 103 us
  Pallas kernels  93.6 us (90%)
  local copies, waits for them, and re-layouts  9.03 us (9%)
    pallas_call x1, Pallas kernels, exchange(): pl.pallas_call(exchange_kernel, out_shape=(jax.ShapeDtypeStruct(q.shape,...  92.7 us
    unnamed x14, local copies, waits for them, and re-layouts  9.03 us

profile of v2, /device:TPU:17, one launch (start us, length us, event | category | flops | bytes accessed | tf_op | source)
XLA Modules:
  0.0 103.3 jit_solution(15403485279566543499)
XLA Ops:
  0.6 0.0 copy-start
  0.6 1.0 copy-done
  1.7 0.0 copy-start.1
  1.7 0.9 copy-done.1
  2.6 0.0 copy-start.2
  2.6 0.7 copy-done.2
  3.3 0.9 shard_map.86.att_ref
  4.2 0.0 copy-start.3
  4.2 1.0 copy-done.3
  5.2 0.0 copy-start.4
  5.2 0.7 copy-done.4
  5.9 0.0 copy-start.5
  5.9 0.7 copy-done.5
  6.6 92.7 %shard_map.87 = (bf16[128,8192]{1,0:T(8,128)(2,1)}, bf16[8,32,2048]{2,1,0:T(8,128)(2,1)S(1)}) custom-call(s32[4]{0:T(128)S(1)} %copy-done.4, s32[1,4]{1,0:T(1,128)S(1)} %copy-done.5, bf16[128,8192]{1,0:T(8,128)(2,1)} %q_ref.3, bf16[128,2048]{1,0:T(8,128)(2,1)S(1)} %copy-done.3, bf16[32,8192]{1,0:T(8,128)(2,1)S(1)} %shard_map.86.att_ref), custom_call_target="tpu_custom_call" | custom-call | flops 9663676416 | bytes 16777216 | tf_op jit(solution)/shard_map/pallas_call | solution.py:453
  99.2 3.1 %copy.11 = bf16[128,8192]{1,0:T(8,128)(2,1)} copy(bf16[128,8192]{1,0:T(8,128)(2,1)} %get-tuple-element.8) | data formatting | bytes 4194304
  102.3 1.0 copy.12
Async XLA Ops:
  0.6 1.0 %copy-start = (bf16[32,8192]{1,0:T(8,128)(2,1)S(1)}, bf16[32,8192]{1,0:T(8,128)(2,1)}, u32[]{:S(2)}) copy-start(bf16[32,8192]{1,0:T(8,128)(2,1)} %q_ref.2) | copy-start | bytes 1572868
  1.7 0.9 copy-start.1
  2.6 0.7 copy-start.2
  4.2 1.0 %copy-start.3 = (bf16[128,2048]{1,0:T(8,128)(2,1)S(1)}, bf16[128,2048]{1,0:T(8,128)(2,1)}, u32[]{:S(2)}) copy-start(bf16[128,2048]{1,0:T(8,128)(2,1)} %kv_ref.3) | copy-start | bytes 1572868
  5.2 0.7 copy-start.4
  5.9 0.7 copy-start.5
